TPU v7x, 128 devices: a whole 4x4x4 slice. The times are simulated.
128 devices in a mesh: ctx: 32 (over x, y, core), head: 4 (over z).
Axes of the slice: x: 4, y: 4, z: 4, core: 2. Of those that a mesh axis runs over, the one named last changes fastest.
Arguments:
- queries: bfloat16 [24576, 2048], P(('ctx', 'head')), may hold values from -9 to 9
- keys: bfloat16 [24576, 2048], P(('ctx', 'head')), may hold values from -9 to 9
- values: bfloat16 [24576, 2048], P(('ctx', 'head')), may hold values from -12 to 12
- grad_out: bfloat16 [24576, 2048], P(('ctx', 'head')), may hold values from -6 to 6
- pattern: int32 [192, 16], replicated, may hold values from -1 to 191, as said below
Outputs:
- attn_out: bfloat16 [24576, 2048], P(('ctx', 'head'))
- grad_query: bfloat16 [24576, 2048], P(('ctx', 'head'))
- grad_key: bfloat16 [24576, 2048], P(('ctx', 'head'))
- grad_value: bfloat16 [24576, 2048], P(('ctx', 'head'))
Inputs may be any that keep to these rules, and one draw needn't show every extreme that they name: `pattern`: row b: entries 0 to 3 are the blocks b - 3 to b in order, -1 where such a number is negative; the remaining entries are, ascending, some of the blocks c <= b - 4 whose remainder modulo 16 equals one phase shared by all rows (each row its own subset, always holding the smallest such block where one exists), followed by -1.
All inputs are finite; a program needn't handle non-finite values.
Results may differ from a plain program's by a relative error of at most 0.015.
Values may be sent and summed in bfloat16 or wider, within the bound.
A program may use at most 128 MiB of HBM per device.

v0:
```python
import math
import jax
import jax.numpy as jnp
from jax import lax
from jax.sharding import PartitionSpec as P

HEAD_DIM = 128
HEAD_DEV = 4
BLOCK = 128
LOCAL = 4
STRIDE = 16
TOK_DEV = 768


def shifted(value, axis, steps):
    count = lax.axis_size(axis)
    first, last = (max(0, -steps), min(count, count - steps))
    return lax.ppermute(value, axis, [(source, source + steps) for source in range(first, last)])


def per_device(queries, keys, values, grad_out, pattern):
    query_here, key_here, value_here, grad_here = (
        lax.all_to_all(queries, "head", split_axis=1, concat_axis=0, tiled=True),
        lax.all_to_all(keys, "head", split_axis=1, concat_axis=0, tiled=True),
        lax.all_to_all(values, "head", split_axis=1, concat_axis=0, tiled=True),
        lax.all_to_all(grad_out, "head", split_axis=1, concat_axis=0, tiled=True),
    )
    device = lax.axis_index("ctx")
    cycle_size = lax.axis_size("ctx")
    blocks_here = TOK_DEV // BLOCK
    block_total = pattern.shape[0]
    strided_count = block_total // STRIDE
    owned_count = (blocks_here + STRIDE - 1) // STRIDE
    features = HEAD_DEV * HEAD_DIM
    score_scale = 1.0 / math.sqrt(HEAD_DIM)
    edge_rows = (LOCAL - 1) * BLOCK
    stride_phase = pattern[block_total - 1, LOCAL] % STRIDE
    first_local = jnp.mod(stride_phase - device * blocks_here, STRIDE)
    own_local = first_local + STRIDE * jnp.arange(owned_count, dtype=jnp.int32)
    own_valid = own_local < blocks_here
    own_safe = jnp.where(own_valid, own_local, 0)
    key_blocks = key_here.reshape(blocks_here, BLOCK, features)
    value_blocks = value_here.reshape(blocks_here, BLOCK, features)
    offer_keys = jnp.where(own_valid[:, None, None], key_blocks[own_safe], 0)
    offer_values = jnp.where(own_valid[:, None, None], value_blocks[own_safe], 0)
    pool_ids = stride_phase + STRIDE * jnp.arange(strided_count, dtype=jnp.int32)
    pool_owner = pool_ids // blocks_here
    slot_within = (pool_ids - pool_owner * blocks_here) // STRIDE
    pool_slots = pool_owner * owned_count + slot_within
    all_keys, all_values = (
        lax.all_gather(
            offer_keys.reshape(owned_count * BLOCK, features), "ctx", axis=0, tiled=True
        ),
        lax.all_gather(
            offer_values.reshape(owned_count * BLOCK, features), "ctx", axis=0, tiled=True
        ),
    )
    pool_keys = all_keys.reshape(cycle_size * owned_count, BLOCK, features)[pool_slots]
    pool_values = all_values.reshape(cycle_size * owned_count, BLOCK, features)[pool_slots]
    before_keys, before_values = shifted(
        (key_here[TOK_DEV - edge_rows :], value_here[TOK_DEV - edge_rows :]), "ctx", 1
    )
    window_keys = jnp.concatenate([before_keys, key_here], 0).reshape(
        edge_rows + TOK_DEV, HEAD_DEV, HEAD_DIM
    )
    window_values = jnp.concatenate([before_values, value_here], 0).reshape(
        edge_rows + TOK_DEV, HEAD_DEV, HEAD_DIM
    )
    pool_keys3 = pool_keys.reshape(strided_count * BLOCK, HEAD_DEV, HEAD_DIM)
    pool_values3 = pool_values.reshape(strided_count * BLOCK, HEAD_DEV, HEAD_DIM)
    my_rows = lax.dynamic_slice_in_dim(pattern, device * blocks_here, blocks_here, 0)
    span_rows = LOCAL * BLOCK
    key_place = jnp.arange(span_rows)
    query_place = jnp.arange(BLOCK)
    last_start = (LOCAL - 1) * BLOCK
    causal = (key_place[None, :] < last_start) | (
        key_place[None, :] - last_start <= query_place[:, None]
    )

    def attend_block(totals, operands):
        key_ext, value_ext, key_pool, value_pool = totals
        block_index, query_block, grad_block, pattern_row = operands
        near_keys = lax.dynamic_slice_in_dim(window_keys, block_index * BLOCK, span_rows, 0)
        near_values = lax.dynamic_slice_in_dim(window_values, block_index * BLOCK, span_rows, 0)
        joined_keys = jnp.concatenate([near_keys, pool_keys3], 0)
        joined_values = jnp.concatenate([near_values, pool_values3], 0)
        near_allowed = jnp.repeat(pattern_row[:LOCAL] >= 0, BLOCK)
        far_allowed = jnp.repeat(
            jnp.any(pattern_row[LOCAL:][None, :] == pool_ids[:, None], axis=1), BLOCK
        )
        allowed = jnp.concatenate(
            [
                causal & near_allowed[None, :],
                jnp.broadcast_to(far_allowed[None, :], (BLOCK, strided_count * BLOCK)),
            ],
            1,
        )
        scores = (
            jnp.einsum("qhd,khd->hqk", query_block, joined_keys, preferred_element_type=jnp.float32)
            * score_scale
        )
        masked = jnp.where(allowed[None], scores, -jnp.inf)
        row_top = jnp.max(masked, axis=2, keepdims=True)
        exponent = jnp.exp(masked - row_top)
        weights_wide = exponent / jnp.sum(exponent, axis=2, keepdims=True)
        weights = weights_wide.astype(jnp.bfloat16)
        output_wide = jnp.einsum(
            "hqk,khd->qhd", weights, joined_values, preferred_element_type=jnp.float32
        )
        grad_weights = jnp.einsum(
            "qhd,khd->hqk", grad_block, joined_values, preferred_element_type=jnp.float32
        )
        row_delta = jnp.sum(grad_block.astype(jnp.float32) * output_wide, axis=2).T[:, :, None]
        grad_scores = (score_scale * weights_wide * (grad_weights - row_delta)).astype(jnp.bfloat16)
        grad_query = jnp.einsum(
            "hqk,khd->qhd", grad_scores, joined_keys, preferred_element_type=jnp.float32
        )
        key_terms = jnp.einsum(
            "hqk,qhd->khd", grad_scores, query_block, preferred_element_type=jnp.float32
        )
        value_terms = jnp.einsum(
            "hqk,qhd->khd", weights, grad_block, preferred_element_type=jnp.float32
        )
        start_row = block_index * BLOCK
        key_ext = lax.dynamic_update_slice_in_dim(
            key_ext,
            lax.dynamic_slice_in_dim(key_ext, start_row, span_rows, 0) + key_terms[:span_rows],
            start_row,
            0,
        )
        value_ext = lax.dynamic_update_slice_in_dim(
            value_ext,
            lax.dynamic_slice_in_dim(value_ext, start_row, span_rows, 0) + value_terms[:span_rows],
            start_row,
            0,
        )
        key_pool = key_pool + key_terms[span_rows:]
        value_pool = value_pool + value_terms[span_rows:]
        return (
            (key_ext, value_ext, key_pool, value_pool),
            (output_wide.astype(jnp.bfloat16), grad_query.astype(jnp.bfloat16)),
        )

    ext_zero = jnp.zeros((edge_rows + TOK_DEV, HEAD_DEV, HEAD_DIM), jnp.float32)
    pool_zero = jnp.zeros((strided_count * BLOCK, HEAD_DEV, HEAD_DIM), jnp.float32)
    operands = (
        jnp.arange(blocks_here, dtype=jnp.int32),
        query_here.reshape(blocks_here, BLOCK, HEAD_DEV, HEAD_DIM),
        grad_here.reshape(blocks_here, BLOCK, HEAD_DEV, HEAD_DIM),
        my_rows,
    )
    (key_ext, value_ext, key_pool, value_pool), (outputs, query_grads) = lax.scan(
        attend_block, (ext_zero, ext_zero, pool_zero, pool_zero), operands
    )
    key_ext = key_ext.reshape(edge_rows + TOK_DEV, features)
    value_ext = value_ext.reshape(edge_rows + TOK_DEV, features)
    back_keys, back_values = (
        shifted(key_ext[:edge_rows].astype(jnp.bfloat16), "ctx", -1).astype(jnp.float32),
        shifted(value_ext[:edge_rows].astype(jnp.bfloat16), "ctx", -1).astype(jnp.float32),
    )
    own_keys = key_ext[edge_rows:] + jnp.pad(back_keys, ((TOK_DEV - edge_rows, 0), (0, 0)))
    own_values = value_ext[edge_rows:] + jnp.pad(back_values, ((TOK_DEV - edge_rows, 0), (0, 0)))
    pool_key_grads = key_pool.reshape(strided_count, BLOCK, features)
    pool_value_grads = value_pool.reshape(strided_count, BLOCK, features)
    slot_keys = (
        jnp.zeros((cycle_size * owned_count, BLOCK, features), jnp.float32)
        .at[pool_slots]
        .set(pool_key_grads)
    )
    slot_values = (
        jnp.zeros((cycle_size * owned_count, BLOCK, features), jnp.float32)
        .at[pool_slots]
        .set(pool_value_grads)
    )
    mine_keys, mine_values = (
        lax.psum_scatter(
            slot_keys.reshape(cycle_size * owned_count * BLOCK, features).astype(jnp.bfloat16),
            "ctx",
            scatter_dimension=0,
            tiled=True,
        ).astype(jnp.float32),
        lax.psum_scatter(
            slot_values.reshape(cycle_size * owned_count * BLOCK, features).astype(jnp.bfloat16),
            "ctx",
            scatter_dimension=0,
            tiled=True,
        ).astype(jnp.float32),
    )
    mine_keys = mine_keys.reshape(owned_count, BLOCK, features)
    mine_values = mine_values.reshape(owned_count, BLOCK, features)
    own_keys = (
        own_keys.reshape(blocks_here, BLOCK, features)
        .at[own_safe]
        .add(jnp.where(own_valid[:, None, None], mine_keys, 0.0))
    )
    own_values = (
        own_values.reshape(blocks_here, BLOCK, features)
        .at[own_safe]
        .add(jnp.where(own_valid[:, None, None], mine_values, 0.0))
    )
    attn_local = outputs.reshape(TOK_DEV, features)
    query_local = query_grads.reshape(TOK_DEV, features)
    key_local = own_keys.reshape(TOK_DEV, features).astype(jnp.bfloat16)
    value_local = own_values.reshape(TOK_DEV, features).astype(jnp.bfloat16)
    attn_out, grad_query, grad_key, grad_value = (
        lax.all_to_all(attn_local, "head", split_axis=0, concat_axis=1, tiled=True),
        lax.all_to_all(query_local, "head", split_axis=0, concat_axis=1, tiled=True),
        lax.all_to_all(key_local, "head", split_axis=0, concat_axis=1, tiled=True),
        lax.all_to_all(value_local, "head", split_axis=0, concat_axis=1, tiled=True),
    )
    return (attn_out, grad_query, grad_key, grad_value)


def solution(mesh):
    placed = (
        P(("ctx", "head"), None),
        P(("ctx", "head"), None),
        P(("ctx", "head"), None),
        P(("ctx", "head"), None),
        P(),
    )
    return jax.shard_map(
        per_device,
        mesh=mesh,
        in_specs=placed,
        out_specs=(
            P(("ctx", "head"), None),
            P(("ctx", "head"), None),
            P(("ctx", "head"), None),
            P(("ctx", "head"), None),
        ),
        check_vma=False,
    )
```

profile of v0, /device:TPU:0, one launch (start us, length us, event | category | flops | bytes accessed | tf_op | source)
XLA Modules:
  0.0 579.7 jit_solution(18047088099131019259)
XLA Ops:
  9.3 5.4 all-to-all-start.1
  17.3 9.7 %all-to-all-done.1 = bf16[192,4,512]{2,0,1:T(8,128)(2,1)S(1)} async-done(((bf16[192,4,512]{2,0,1:T(8,128)(2,1)}), bf16[192,4,512]{2,0,1:T(8,128)(2,1)S(1)}, u32[]{:S(2)}, u32[]{:S(2)}) %all-to-all-start.1) | async-done | bytes 786464 | tf_op jit(solution)/shard_map/all_to_all | solution.py:24
  27.9 13.9 %all_to_all.134 = bf16[192,4,512]{2,0,1:T(8,128)(2,1)S(1)} all-to-all(bf16[192,4,512]{2,0,1:T(8,128)(2,1)S(1)} %bitcast.174), channel_id=1, replica_groups=mesh['ctx'=32,'head'=4] {'head'}, dimensions={1} | all-to-all | bytes 1572864 | tf_op jit(solution)/shard_map/all_to_all | solution.py:25
  43.4 3.5 all-to-all-start
  47.9 9.4 %all-to-all-done = bf16[192,4,512]{2,0,1:T(8,128)(2,1)S(1)} async-done(((bf16[192,4,512]{2,0,1:T(8,128)(2,1)}), bf16[192,4,512]{2,0,1:T(8,128)(2,1)S(1)}, u32[]{:S(2)}, u32[]{:S(2)}) %all-to-all-start) | async-done | bytes 786464 | tf_op jit(solution)/shard_map/all_to_all | solution.py:23
  57.4 3.5 all-to-all-start.2
  65.3 3.5 collective-permute-start.1
  75.1 4.9 pad_maximum_fusion
  80.0 5.7 pad_maximum_fusion.1
  85.8 4.0 gather_fusion
  93.6 27.4 %all-gather.7.cloned.1.call-done = bf16[1,4096,512]{2,1,0:T(8,128)(2,1)} async-done(((bf16[1,128,512]{2,1,0:T(8,128)(2,1)}), bf16[1,4096,512]{2,1,0:T(8,128)(2,1)}) %all-gather.7.cloned.1.call-update) | async-done | bytes 4194320 | tf_op jit(solution)/shard_map/all_gather | solution.py:54
  121.0 4.0 gather_fusion.1
  131.9 219.7 %while.25 = (s32[]{:T(128)}, f32[1152,4,128]{0,2,1:T(8,128)}, f32[1152,4,128]{0,2,1:T(8,128)}, f32[1536,4,128]{0,2,1:T(8,128)}, f32[1536,4,128]{0,2,1:T(8,128)},...) while((s32[]{:T(128)}, f32[1152,4,128]{0,2,1:T(8,128)}, ...), condition=%wide.region_5.6_spmd.clone, body=%wide.region_0.5_spmd.clone.sunk | while | flops 1626605312 | bytes 194795088 | solution.py:152
  141.6 3.4 fusion.54
  145.0 2.8 fusion.55
  159.6 3.5 fusion.56
  178.2 3.4 fusion.54
  181.6 2.8 fusion.55
  196.2 3.6 fusion.56
  214.8 3.4 fusion.54
  218.2 2.8 fusion.55
  232.8 3.6 fusion.56
  251.4 3.4 fusion.54
  254.9 2.8 fusion.55
  269.5 3.6 fusion.56
  288.1 3.4 fusion.54
  291.5 2.8 fusion.55
  306.1 3.6 fusion.56
  324.7 3.4 fusion.54
  342.7 3.6 fusion.56
  351.6 3.2 copy.143
  354.9 2.9 reshape.381
  357.7 4.3 broadcast.237.clone
  362.1 6.1 %scatter_fusion = f32[32,128,512]{2,1,0:T(8,128)} fusion(f32[32,128,512]{2,1,0:T(8,128)} %broadcast.237.clone, s32[12]{0:T(128)S(1)} %fusion.22, f32[12,128,512]{2,1,0:T(8,128)S(1)} %copy-done.11), kind=kCustom, calls=%fused_computation.2 | custom fusion | bytes 9437232 | tf_op jit(solution)/shard_map/scatter | solution.py:168
  368.2 6.0 %convert_element_type.67 = bf16[32,128,512]{2,1,0:T(8,128)(2,1)} convert(f32[32,128,512]{2,1,0:T(8,128)} %scatter_fusion) | non-fusion elementwise | flops 2097152 | bytes 12582912 | tf_op jit(solution)/shard_map/convert_element_type | solution.py:177
  376.1 2.8 copy.147
  378.9 3.3 reshape.389
  382.2 4.3 broadcast.237.clone.1
  386.6 6.3 %scatter_fusion.1 = f32[32,128,512]{2,1,0:T(8,128)} fusion(f32[32,128,512]{2,1,0:T(8,128)} %broadcast.237.clone.1, s32[12]{0:T(128)S(1)} %fusion.22, f32[12,128,512]{2,1,0:T(8,128)S(1)} %reshape.389), kind=kCustom, calls=%fused_computation.3 | custom fusion | bytes 9437232 | tf_op jit(solution)/shard_map/scatter | solution.py:173
  392.8 6.2 %convert_element_type.73 = bf16[32,128,512]{2,1,0:T(8,128)(2,1)} convert(f32[32,128,512]{2,1,0:T(8,128)} %scatter_fusion.1) | non-fusion elementwise | flops 2097152 | bytes 12582912 | tf_op jit(solution)/shard_map/convert_element_type | solution.py:183
  401.3 4.5 all-to-all-start.5
  422.8 4.7 all-to-all-start.4
  429.3 27.1 %reduce-scatter.3.cloned.1.call-done = bf16[128,512]{1,0:T(8,128)(2,1)} async-done(((bf16[4096,512]{1,0:T(8,128)(2,1)}), bf16[128,512]{1,0:T(8,128)(2,1)}) %reduce-scatter.3.cloned.1.call-update) | async-done | bytes 131088 | tf_op jit(solution)/shard_map/reduce_scatter | solution.py:176
  456.4 85.2 %reduce-scatter.5.cloned.1.call-done = bf16[128,512]{1,0:T(8,128)(2,1)} async-done(((bf16[4096,512]{1,0:T(8,128)(2,1)}), bf16[128,512]{1,0:T(8,128)(2,1)}) %reduce-scatter.5.cloned.1.call-update) | async-done | bytes 131088 | tf_op jit(solution)/shard_map/reduce_scatter | solution.py:182
  544.2 4.4 all-to-all-start.6
  549.6 9.7 %all-to-all-done.6 = bf16[4,192,512]{2,1,0:T(8,128)(2,1)S(1)} async-done(((bf16[4,192,512]{2,1,0:T(8,128)(2,1)}), bf16[4,192,512]{2,1,0:T(8,128)(2,1)S(1)}, u32[]{:S(2)}, u32[]{:S(2)}) %all-to-all-start.6) | async-done | bytes 786464 | tf_op jit(solution)/shard_map/all_to_all | solution.py:208
  559.3 3.5 all-to-all-start.7
  568.0 4.3 all-to-all-done.7
  (402 shorter events, 218.9 us)
Async XLA Ops:
  7.2 7.6 %copy-start.21 = (s32[192,16]{0,1:T(8,128)S(1)}, s32[192,16]{0,1:T(8,128)}, u32[]{:S(2)}) copy-start(s32[192,16]{0,1:T(8,128)} %param.15) | copy-start | bytes 36868
  7.2 20.6 %copy-start.16 = (bf16[192,2048]{1,0:T(8,128)(2,1)S(1)}, bf16[192,2048]{1,0:T(8,128)(2,1)}, u32[]{:S(2)}) copy-start(bf16[192,2048]{1,0:T(8,128)(2,1)} %param.13) | copy-start | bytes 2359300
  9.3 17.7 %all-to-all-start.1 = ((bf16[192,4,512]{2,0,1:T(8,128)(2,1)}), bf16[192,4,512]{2,0,1:T(8,128)(2,1)S(1)}, u32[]{:S(2)}, u32[]{:S(2)}) async-start(bf16[192,4,512]{2,0,1:T(8,128)(2,1)} %bitcast.108), calls=%async_computation.1 | async-start | bytes 1572864 | tf_op jit(solution)/shard_map/all_to_all | solution.py:24
  14.7 27.7 %copy-start.17 = (bf16[192,2048]{1,0:T(8,128)(2,1)S(1)}, bf16[192,2048]{1,0:T(8,128)(2,1)}, u32[]{:S(2)}) copy-start(bf16[192,2048]{1,0:T(8,128)(2,1)} %param.11) | copy-start | bytes 2359300
  14.7 71.0 %all-gather.5.cloned.1.call-start = ((), (), s32[]{:S(2)}) async-start(), calls=%async_computation.12 | async-start | bytes 4325376 | tf_op jit(solution)/shard_map/all_gather | solution.py:51
  27.7 93.3 %all-gather.7.cloned.1.call-start = ((), (), s32[]{:S(2)}) async-start(), calls=%async_computation.13 | async-start | bytes 4325376 | tf_op jit(solution)/shard_map/all_gather | solution.py:54
  27.8 19.1 %copy-start.18 = (bf16[192,2048]{1,0:T(8,128)(2,1)S(1)}, bf16[192,2048]{1,0:T(8,128)(2,1)}, u32[]{:S(2)}) copy-start(bf16[192,2048]{1,0:T(8,128)(2,1)} %param.14) | copy-start | bytes 2359300
  43.4 13.9 %all-to-all-start = ((bf16[192,4,512]{2,0,1:T(8,128)(2,1)}), bf16[192,4,512]{2,0,1:T(8,128)(2,1)S(1)}, u32[]{:S(2)}, u32[]{:S(2)}) async-start(bf16[192,4,512]{2,0,1:T(8,128)(2,1)} %bitcast.109), calls=%async_computation | async-start | bytes 1572864 | tf_op jit(solution)/shard_map/all_to_all | solution.py:23
  57.4 14.7 %all-to-all-start.2 = ((bf16[192,4,512]{2,0,1:T(8,128)(2,1)}), bf16[192,4,512]{2,0,1:T(8,128)(2,1)S(1)}, u32[]{:S(2)}, u32[]{:S(2)}) async-start(bf16[192,4,512]{2,0,1:T(8,128)(2,1)} %bitcast.107), calls=%async_computation.2 | async-start | bytes 1572864 | tf_op jit(solution)/shard_map/all_to_all | solution.py:26
  60.9 395.5 %reduce-scatter.3.cloned.1.call-start = ((), (), s32[]{:S(2)}) async-start(), calls=%async_computation.10 | async-start | bytes 4325376 | tf_op jit(solution)/shard_map/reduce_scatter | solution.py:176
  62.4 10.6 %collective-permute-start = (bf16[384,512]{1,0:T(8,128)(2,1)}, bf16[384,512]{1,0:T(8,128)(2,1)}, u32[]{:S(2)}, u32[]{:S(2)}) collective-permute-start(bf16[384,512]{1,0:T(8,128)(2,1)} %bitcast.2), channel_id=1, source_target_pairs={{0,4},{4,8},{8,12},{12,16},{16,20},{20,24},{24,28},{28,32},{32,36}... | collective-permute-start | bytes 1179656 | tf_op jit(solution)/shard_map/ppermute | solution.py:18
  65.3 9.4 %collective-permute-start.1 = (bf16[384,512]{1,0:T(8,128)(2,1)}, bf16[384,512]{1,0:T(8,128)(2,1)S(1)}, u32[]{:S(2)}, u32[]{:S(2)}) collective-permute-start(bf16[384,512]{1,0:T(8,128)(2,1)} %bitcast.13), channel_id=1, source_target_pairs={{0,4},{4,8},{8,12},{12,16},{16,20},{20,24},{24,28},{28,32},{32,36}... | collective-permute-start | bytes 1179656 | tf_op jit(solution)/shard_map/ppermute | solution.py:18
  74.4 5.6 copy-start.14
  131.9 5.9 %copy-start.12 = (bf16[1152,4,128]{2,1,0:T(4,128)(2,1)}, bf16[1152,4,128]{2,1,0:T(4,128)(2,1)S(1)}, u32[]{:S(2)}) copy-start(bf16[1152,4,128]{2,1,0:T(4,128)(2,1)S(1)} %get-tuple-element.535) | copy-start | bytes 3538948 | tf_op jit(solution)/shard_map/while
  133.2 4.9 copy-start.9
  138.3 6.7 %copy-start.7 = (bf16[2048,4,128]{2,0,1:T(8,128)(2,1)}, bf16[2048,4,128]{2,0,1:T(8,128)(2,1)S(1)}, u32[]{:S(2)}) copy-start(bf16[2048,4,128]{2,0,1:T(8,128)(2,1)S(1)} %constant_dynamic-update-slice_fusion.5) | copy-start | bytes 6291460 | tf_op jit(solution)/shard_map/while
  159.6 4.2 copy-start.4
  163.7 4.8 copy-start.13
  168.5 5.9 %copy-start.12 = (bf16[1152,4,128]{2,1,0:T(4,128)(2,1)}, bf16[1152,4,128]{2,1,0:T(4,128)(2,1)S(1)}, u32[]{:S(2)}) copy-start(bf16[1152,4,128]{2,1,0:T(4,128)(2,1)S(1)} %get-tuple-element.535) | copy-start | bytes 3538948 | tf_op jit(solution)/shard_map/while
  169.9 4.9 copy-start.9
  175.0 6.7 %copy-start.7 = (bf16[2048,4,128]{2,0,1:T(8,128)(2,1)}, bf16[2048,4,128]{2,0,1:T(8,128)(2,1)S(1)}, u32[]{:S(2)}) copy-start(bf16[2048,4,128]{2,0,1:T(8,128)(2,1)S(1)} %constant_dynamic-update-slice_fusion.5) | copy-start | bytes 6291460 | tf_op jit(solution)/shard_map/while
  196.2 4.2 copy-start.4
  200.4 4.8 copy-start.13
  205.1 5.9 %copy-start.12 = (bf16[1152,4,128]{2,1,0:T(4,128)(2,1)}, bf16[1152,4,128]{2,1,0:T(4,128)(2,1)S(1)}, u32[]{:S(2)}) copy-start(bf16[1152,4,128]{2,1,0:T(4,128)(2,1)S(1)} %get-tuple-element.535) | copy-start | bytes 3538948 | tf_op jit(solution)/shard_map/while
  206.5 4.9 copy-start.9
  211.6 6.7 %copy-start.7 = (bf16[2048,4,128]{2,0,1:T(8,128)(2,1)}, bf16[2048,4,128]{2,0,1:T(8,128)(2,1)S(1)}, u32[]{:S(2)}) copy-start(bf16[2048,4,128]{2,0,1:T(8,128)(2,1)S(1)} %constant_dynamic-update-slice_fusion.5) | copy-start | bytes 6291460 | tf_op jit(solution)/shard_map/while
  237.0 4.8 copy-start.13
  241.8 5.9 %copy-start.12 = (bf16[1152,4,128]{2,1,0:T(4,128)(2,1)}, bf16[1152,4,128]{2,1,0:T(4,128)(2,1)S(1)}, u32[]{:S(2)}) copy-start(bf16[1152,4,128]{2,1,0:T(4,128)(2,1)S(1)} %get-tuple-element.535) | copy-start | bytes 3538948 | tf_op jit(solution)/shard_map/while
  243.1 4.9 copy-start.9
  248.2 6.7 %copy-start.7 = (bf16[2048,4,128]{2,0,1:T(8,128)(2,1)}, bf16[2048,4,128]{2,0,1:T(8,128)(2,1)S(1)}, u32[]{:S(2)}) copy-start(bf16[2048,4,128]{2,0,1:T(8,128)(2,1)S(1)} %constant_dynamic-update-slice_fusion.5) | copy-start | bytes 6291460 | tf_op jit(solution)/shard_map/while
  273.6 4.8 copy-start.13
  278.4 5.9 %copy-start.12 = (bf16[1152,4,128]{2,1,0:T(4,128)(2,1)}, bf16[1152,4,128]{2,1,0:T(4,128)(2,1)S(1)}, u32[]{:S(2)}) copy-start(bf16[1152,4,128]{2,1,0:T(4,128)(2,1)S(1)} %get-tuple-element.535) | copy-start | bytes 3538948 | tf_op jit(solution)/shard_map/while
  279.7 4.9 copy-start.9
  284.8 6.7 %copy-start.7 = (bf16[2048,4,128]{2,0,1:T(8,128)(2,1)}, bf16[2048,4,128]{2,0,1:T(8,128)(2,1)S(1)}, u32[]{:S(2)}) copy-start(bf16[2048,4,128]{2,0,1:T(8,128)(2,1)S(1)} %constant_dynamic-update-slice_fusion.5) | copy-start | bytes 6291460 | tf_op jit(solution)/shard_map/while
  310.2 4.8 copy-start.13
  315.0 5.9 %copy-start.12 = (bf16[1152,4,128]{2,1,0:T(4,128)(2,1)}, bf16[1152,4,128]{2,1,0:T(4,128)(2,1)S(1)}, u32[]{:S(2)}) copy-start(bf16[1152,4,128]{2,1,0:T(4,128)(2,1)S(1)} %get-tuple-element.535) | copy-start | bytes 3538948 | tf_op jit(solution)/shard_map/while
  316.3 4.9 copy-start.9
  321.4 6.7 %copy-start.7 = (bf16[2048,4,128]{2,0,1:T(8,128)(2,1)}, bf16[2048,4,128]{2,0,1:T(8,128)(2,1)S(1)}, u32[]{:S(2)}) copy-start(bf16[2048,4,128]{2,0,1:T(8,128)(2,1)S(1)} %constant_dynamic-update-slice_fusion.5) | copy-start | bytes 6291460 | tf_op jit(solution)/shard_map/while
  346.9 4.8 copy-start.13
  357.7 4.3 copy-start.11
  374.3 167.3 %reduce-scatter.5.cloned.1.call-start = ((), (), s32[]{:S(2)}) async-start(), calls=%async_computation.11 | async-start | bytes 4325376 | tf_op jit(solution)/shard_map/reduce_scatter | solution.py:182
  401.3 11.4 %copy-start.22 = (s32[3]{0:T(128)S(1)}, s32[3]{0:T(128)}, u32[]{:S(2)}) copy-start(s32[3]{0:T(128)} %constant.137.clone.1) | copy-start | bytes 40
  401.3 21.4 %all-to-all-start.5 = ((bf16[4,192,512]{2,1,0:T(8,128)(2,1)}), bf16[4,192,512]{2,1,0:T(8,128)(2,1)}, u32[]{:S(2)}, u32[]{:S(2)}) async-start(bf16[4,192,512]{2,1,0:T(8,128)(2,1)} %all_to_all.116), calls=%async_computation.5 | async-start | bytes 1572864 | tf_op jit(solution)/shard_map/all_to_all | solution.py:207
  408.0 19.5 %collective-permute-start.3 = (bf16[384,512]{1,0:T(8,128)(2,1)}, bf16[384,512]{1,0:T(8,128)(2,1)S(1)}, u32[]{:S(2)}, u32[]{:S(2)}) collective-permute-start(bf16[384,512]{1,0:T(8,128)(2,1)} %copy.157), channel_id=1, source_target_pairs={{4,0},{8,4},{12,8},{16,12},{20,16},{24,20},{28,24},{32,28},{36,32}... | collective-permute-start | bytes 1179656 | tf_op jit(solution)/shard_map/ppermute | solution.py:18
  411.4 16.2 %collective-permute-start.2 = (bf16[384,512]{1,0:T(8,128)(2,1)}, bf16[384,512]{1,0:T(8,128)(2,1)}, u32[]{:S(2)}, u32[]{:S(2)}) collective-permute-start(bf16[384,512]{1,0:T(8,128)(2,1)} %copy.155), channel_id=1, source_target_pairs={{4,0},{8,4},{12,8},{16,12},{20,16},{24,20},{28,24},{32,28},{36,32}... | collective-permute-start | bytes 1179656 | tf_op jit(solution)/shard_map/ppermute | solution.py:18
  422.8 121.4 %all-to-all-start.4 = ((bf16[4,192,512]{2,1,0:T(8,128)(2,1)}), bf16[4,192,512]{2,1,0:T(8,128)(2,1)}, u32[]{:S(2)}, u32[]{:S(2)}) async-start(bf16[4,192,512]{2,1,0:T(8,128)(2,1)} %all_to_all.112), calls=%async_computation.4 | async-start | bytes 1572864 | tf_op jit(solution)/shard_map/all_to_all | solution.py:206
  544.2 15.1 %all-to-all-start.6 = ((bf16[4,192,512]{2,1,0:T(8,128)(2,1)}), bf16[4,192,512]{2,1,0:T(8,128)(2,1)S(1)}, u32[]{:S(2)}, u32[]{:S(2)}) async-start(bf16[4,192,512]{2,1,0:T(8,128)(2,1)} %bitcast.175), calls=%async_computation.7 | async-start | bytes 1572864 | tf_op jit(solution)/shard_map/all_to_all | solution.py:208
  559.3 13.0 %all-to-all-start.7 = ((bf16[4,192,512]{2,1,0:T(8,128)(2,1)}), bf16[4,192,512]{2,1,0:T(8,128)(2,1)S(1)}, u32[]{:S(2)}, u32[]{:S(2)}) async-start(bf16[4,192,512]{2,1,0:T(8,128)(2,1)} %bitcast.31), calls=%async_computation.9 | async-start | bytes 1572864 | tf_op jit(solution)/shard_map/all_to_all | solution.py:209
  (50 other events, 132.3 us)
Sparse Core Ops, SparseCore 0:
  27.8 45.4 all-gather.4
  75.6 45.3 all-gather.6
  374.4 81.9 reduce-scatter.2
  460.3 81.1 reduce-scatter.4
where the time goes:
time: 583 us; the launch traced here: 580 us
  local copies, waits for them, and re-layouts  176 us (30%)
  waiting for transfers between devices  173 us (30%)
  other arithmetic  83.8 us (14%)
  matrix products  74.7 us (13%)
  starting transfers between devices  37.7 us (6%)
  between operations  16.1 us (3%)
  blocking collectives  13.9 us (2%)
    reduce_scatter x1, waiting for transfers between devices, per_device(): lax.psum_scatter(slot_values.reshape(cycle_size * owned_count * BLOCK, fe...  85.2 us
    while x156, local copies, waits for them, and re-layouts  40.2 us
    all_gather x1, waiting for transfers between devices, per_device(): lax.all_gather(offer_values.reshape(owned_count * BLOCK, features), 'ctx'...  27.4 us
    reduce_scatter x1, waiting for transfers between devices, per_device(): lax.psum_scatter(slot_keys.reshape(cycle_size * owned_count * BLOCK, feat...  27.1 us
    dynamic_update_slice x6, other arithmetic, attend_block(): lax.dynamic_update_slice_in_dim(value_ext, lax.dynamic_slice_in_dim(value...  21.6 us
    sub x6, matrix products, attend_block(): exponent = jnp.exp(masked - row_top)  20.4 us
    dynamic_slice x24, local copies, waits for them, and re-layouts, per_device(): lax.scan(attend_block, (ext_zero, ext_zero, pool_zero, pool_zero), operands)  20.3 us
    convert_element_type x6, other arithmetic, attend_block(): weights = weights_wide.astype(jnp.bfloat16)  16.7 us
  transfers between devices with their start and end apart: 15, of which 7 were waited for; matrix products, arithmetic and copies ran while one was open for 13% of the time, Pallas kernels for 0%

commit v1 on v0

--- a/solution.py
+++ b/solution.py
@@ -51,8 +51,16 @@
         lax.all_gather(
             offer_keys.reshape(owned_count * BLOCK, features), "ctx", axis=0, tiled=True
         ),
-        lax.all_gather(
-            offer_values.reshape(owned_count * BLOCK, features), "ctx", axis=0, tiled=True
+        jnp.concatenate(
+            lax.all_to_all(
+                jnp.stack(
+                    [offer_values.reshape(owned_count * BLOCK, features)] * lax.axis_size("ctx")
+                ),
+                "ctx",
+                0,
+                0,
+            ),
+            axis=0,
         ),
     )
     pool_keys = all_keys.reshape(cycle_size * owned_count, BLOCK, features)[pool_slots]

time: 583 us -> 618 us (1.060)
  waiting for transfers between devices: 173 us -> 207 us
  blocking collectives: 13.9 us -> 0 us
  starting transfers between devices: 37.7 us -> 48.8 us
    all_to_all x0 -> x2, waiting for transfers between devices: none -> 35.7 us  [the longest x1 27.7 us: per_device(): lax.all_to_all(jnp.stack([offer_values.reshape(owned_count * BLOCK, featu...]
    all_gather x1 -> x0, waiting for transfers between devices: 27.4 us -> none  [per_device(): lax.all_gather(offer_values.reshape(owned_count * BLOCK, features), 'ctx'...]
    all_to_all x1 -> x0, blocking collectives: 13.9 us -> none  [per_device(): lax.all_to_all(values, 'head', split_axis=1, concat_axis=0, tiled=True)]
    reduce_scatter x1, waiting for transfers between devices: 27.1 us -> 39.6 us  [per_device(): lax.psum_scatter(slot_keys.reshape(cycle_size * owned_count * BLOCK, feat...]
    all_to_all x0 -> x2, starting transfers between devices: none -> 11 us  [the longest x1 7.46 us: per_device(): lax.all_to_all(jnp.stack([offer_values.reshape(owned_count * BLOCK, featu...]
    all_to_all x1, waiting for transfers between devices: 0.01 us -> 9.43 us  [per_device(): lax.all_to_all(grad_out, 'head', split_axis=1, concat_axis=0, tiled=True)]
  transfers between devices with their start and end apart: 15 -> 16, of which waited for: 7 -> 10; matrix products, arithmetic and copies ran while one was open for 13% -> 13% of each run, Pallas kernels for 0% -> 0%
where the time goes in v1:
time: 618 us; the launch traced here: 615 us
  waiting for transfers between devices  207 us (33%)
  local copies, waits for them, and re-layouts  180 us (29%)
  other arithmetic  82.9 us (13%)
  matrix products  74.7 us (12%)
  starting transfers between devices  48.8 us (8%)
  between operations  16.1 us (3%)
    reduce_scatter x1, waiting for transfers between devices, per_device(): lax.psum_scatter(slot_values.reshape(cycle_size * owned_count * BLOCK, fe...  85.3 us
    while x156, local copies, waits for them, and re-layouts  40.1 us
    reduce_scatter x1, waiting for transfers between devices, per_device(): lax.psum_scatter(slot_keys.reshape(cycle_size * owned_count * BLOCK, feat...  39.6 us
    all_to_all x1, waiting for transfers between devices, per_device(): lax.all_to_all(jnp.stack([offer_values.reshape(owned_count * BLOCK, featu...  27.7 us
    dynamic_update_slice x6, other arithmetic, attend_block(): lax.dynamic_update_slice_in_dim(value_ext, lax.dynamic_slice_in_dim(value...  21.4 us
    sub x6, matrix products, attend_block(): exponent = jnp.exp(masked - row_top)  20.4 us
    dynamic_slice x24, local copies, waits for them, and re-layouts, per_device(): lax.scan(attend_block, (ext_zero, ext_zero, pool_zero, pool_zero), operands)  20.3 us
    convert_element_type x6, other arithmetic, attend_block(): weights = weights_wide.astype(jnp.bfloat16)  16.7 us
  transfers between devices with their start and end apart: 16, of which 10 were waited for; matrix products, arithmetic and copies ran while one was open for 13% of the time, Pallas kernels for 0%

profile of v1, /device:TPU:0, one launch (start us, length us, event | category | flops | bytes accessed | tf_op | source)
XLA Modules:
  0.0 614.6 jit_solution(9866771133390272224)
XLA Ops:
  9.3 5.5 all-to-all-start.1
  17.4 9.7 %all-to-all-done.1 = bf16[192,4,512]{2,0,1:T(8,128)(2,1)S(1)} async-done(((bf16[192,4,512]{2,0,1:T(8,128)(2,1)}), bf16[192,4,512]{2,0,1:T(8,128)(2,1)S(1)}, u32[]{:S(2)}, u32[]{:S(2)}) %all-to-all-start.1) | async-done | bytes 786464 | tf_op jit(solution)/shard_map/all_to_all | solution.py:24
  28.8 3.5 all-to-all-start
  33.3 10.4 %all-to-all-done = bf16[192,4,512]{2,0,1:T(8,128)(2,1)S(1)} async-done(((bf16[192,4,512]{2,0,1:T(8,128)(2,1)}), bf16[192,4,512]{2,0,1:T(8,128)(2,1)S(1)}, u32[]{:S(2)}, u32[]{:S(2)}) %all-to-all-start) | async-done | bytes 786464 | tf_op jit(solution)/shard_map/all_to_all | solution.py:23
  43.6 3.5 all-to-all-start.3
  49.3 8.0 %all-to-all-done.3 = bf16[192,4,512]{2,0,1:T(8,128)(2,1)S(1)} async-done(((bf16[192,4,512]{2,0,1:T(8,128)(2,1)}), bf16[192,4,512]{2,0,1:T(8,128)(2,1)S(1)}, u32[]{:S(2)}, u32[]{:S(2)}) %all-to-all-start.3) | async-done | bytes 786464 | tf_op jit(solution)/shard_map/all_to_all | solution.py:25
  57.3 3.5 all-to-all-start.2
  60.8 9.4 %all-to-all-done.2 = bf16[192,4,512]{2,0,1:T(8,128)(2,1)S(1)} async-done(((bf16[192,4,512]{2,0,1:T(8,128)(2,1)}), bf16[192,4,512]{2,0,1:T(8,128)(2,1)S(1)}, u32[]{:S(2)}, u32[]{:S(2)}) %all-to-all-start.2) | async-done | bytes 786464 | tf_op jit(solution)/shard_map/all_to_all | solution.py:26
  72.7 7.5 %all-to-all-start.4 = ((bf16[32,128,512]{2,1,0:T(8,128)(2,1)}), bf16[32,128,512]{2,1,0:T(8,128)(2,1)}, u32[]{:S(2)}, u32[]{:S(2)}) async-start(bf16[32,128,512]{2,1,0:T(8,128)(2,1)} %stack.3), calls=%async_computation.4 | async-start | bytes 8388608 | tf_op jit(solution)/shard_map/all_to_all | solution.py:55
  81.8 2.8 collective-permute-start
  85.4 2.8 collective-permute-start.1
  94.6 4.9 pad_maximum_fusion
  99.5 5.7 pad_maximum_fusion.1
  105.2 27.7 %all-to-all-done.4 = bf16[32,128,512]{2,1,0:T(8,128)(2,1)} async-done(((bf16[32,128,512]{2,1,0:T(8,128)(2,1)}), bf16[32,128,512]{2,1,0:T(8,128)(2,1)}, u32[]{:S(2)}, u32[]{:S(2)}) %all-to-all-start.4) | async-done | bytes 4194336 | tf_op jit(solution)/shard_map/all_to_all | solution.py:55
  133.0 4.1 gather_fusion.1
  140.7 4.0 gather_fusion
  151.7 219.5 %while.25 = (s32[]{:T(128)}, f32[1152,4,128]{0,2,1:T(8,128)}, f32[1152,4,128]{0,2,1:T(8,128)}, f32[1536,4,128]{0,2,1:T(8,128)}, f32[1536,4,128]{0,2,1:T(8,128)},...) while((s32[]{:T(128)}, f32[1152,4,128]{0,2,1:T(8,128)}, ...), condition=%wide.region_5.6_spmd.clone, body=%wide.region_0.5_spmd.clone.sunk | while | flops 1626605312 | bytes 194795088 | solution.py:160
  161.4 3.4 fusion.55
  179.3 3.6 fusion.57
  197.9 3.4 fusion.55
  215.9 3.6 fusion.57
  234.5 3.4 fusion.55
  252.5 3.5 fusion.57
  271.1 3.4 fusion.55
  289.1 3.6 fusion.57
  307.7 3.4 fusion.55
  325.6 3.5 fusion.57
  344.3 3.4 fusion.55
  362.2 3.5 fusion.57
  371.2 3.2 copy.143
  374.4 2.9 reshape.377
  377.3 4.3 broadcast.238.clone
  381.6 6.1 scatter_fusion
  387.7 6.0 convert_element_type.67
  395.6 2.8 copy.147
  398.4 3.3 reshape.385
  401.7 4.3 broadcast.238.clone.1
  406.1 6.1 scatter_fusion.1
  412.2 5.9 convert_element_type.73
  420.5 4.3 all-to-all-start.6
  441.7 4.7 all-to-all-start.5
  446.6 3.2 collective-permute-done.2
  451.5 39.6 %reduce-scatter.3.cloned.1.call-done = bf16[128,512]{1,0:T(8,128)(2,1)} async-done(((bf16[4096,512]{1,0:T(8,128)(2,1)}), bf16[128,512]{1,0:T(8,128)(2,1)}) %reduce-scatter.3.cloned.1.call-update) | async-done | bytes 131088 | tf_op jit(solution)/shard_map/reduce_scatter | solution.py:184
  491.0 85.3 %reduce-scatter.5.cloned.1.call-done = bf16[128,512]{1,0:T(8,128)(2,1)} async-done(((bf16[4096,512]{1,0:T(8,128)(2,1)}), bf16[128,512]{1,0:T(8,128)(2,1)}) %reduce-scatter.5.cloned.1.call-update) | async-done | bytes 131088 | tf_op jit(solution)/shard_map/reduce_scatter | solution.py:190
  579.1 4.4 all-to-all-start.7
  584.5 9.7 %all-to-all-done.7 = bf16[4,192,512]{2,1,0:T(8,128)(2,1)S(1)} async-done(((bf16[4,192,512]{2,1,0:T(8,128)(2,1)}), bf16[4,192,512]{2,1,0:T(8,128)(2,1)S(1)}, u32[]{:S(2)}, u32[]{:S(2)}) %all-to-all-start.7) | async-done | bytes 786464 | tf_op jit(solution)/shard_map/all_to_all | solution.py:216
  594.2 3.5 all-to-all-start.8
  602.9 4.3 all-to-all-done.8
  (401 shorter events, 234.6 us)
Async XLA Ops:
  7.2 7.7 %copy-start.20 = (s32[192,16]{0,1:T(8,128)S(1)}, s32[192,16]{0,1:T(8,128)}, u32[]{:S(2)}) copy-start(s32[192,16]{0,1:T(8,128)} %param.15) | copy-start | bytes 36868
  7.2 20.7 %copy-start.16 = (bf16[192,2048]{1,0:T(8,128)(2,1)S(1)}, bf16[192,2048]{1,0:T(8,128)(2,1)}, u32[]{:S(2)}) copy-start(bf16[192,2048]{1,0:T(8,128)(2,1)} %param.11) | copy-start | bytes 2359300
  9.3 23.0 %copy-start.17 = (bf16[192,2048]{1,0:T(8,128)(2,1)S(1)}, bf16[192,2048]{1,0:T(8,128)(2,1)}, u32[]{:S(2)}) copy-start(bf16[192,2048]{1,0:T(8,128)(2,1)} %param.13) | copy-start | bytes 2359300
  9.3 17.8 %all-to-all-start.1 = ((bf16[192,4,512]{2,0,1:T(8,128)(2,1)}), bf16[192,4,512]{2,0,1:T(8,128)(2,1)S(1)}, u32[]{:S(2)}, u32[]{:S(2)}) async-start(bf16[192,4,512]{2,0,1:T(8,128)(2,1)} %bitcast.109), calls=%async_computation.1 | async-start | bytes 1572864 | tf_op jit(solution)/shard_map/all_to_all | solution.py:24
  14.9 125.9 %all-gather.3.cloned.1.call-start = ((), (), s32[]{:S(2)}) async-start(), calls=%async_computation.13 | async-start | bytes 4325376 | tf_op jit(solution)/shard_map/all_gather | solution.py:51
  28.8 14.8 %all-to-all-start = ((bf16[192,4,512]{2,0,1:T(8,128)(2,1)}), bf16[192,4,512]{2,0,1:T(8,128)(2,1)S(1)}, u32[]{:S(2)}, u32[]{:S(2)}) async-start(bf16[192,4,512]{2,0,1:T(8,128)(2,1)} %bitcast.110), calls=%async_computation | async-start | bytes 1572864 | tf_op jit(solution)/shard_map/all_to_all | solution.py:23
  43.6 13.6 %all-to-all-start.3 = ((bf16[192,4,512]{2,0,1:T(8,128)(2,1)}), bf16[192,4,512]{2,0,1:T(8,128)(2,1)S(1)}, u32[]{:S(2)}, u32[]{:S(2)}) async-start(bf16[192,4,512]{2,0,1:T(8,128)(2,1)} %bitcast.107), calls=%async_computation.3 | async-start | bytes 1572864 | tf_op jit(solution)/shard_map/all_to_all | solution.py:25
  57.3 13.0 %all-to-all-start.2 = ((bf16[192,4,512]{2,0,1:T(8,128)(2,1)}), bf16[192,4,512]{2,0,1:T(8,128)(2,1)S(1)}, u32[]{:S(2)}, u32[]{:S(2)}) async-start(bf16[192,4,512]{2,0,1:T(8,128)(2,1)} %bitcast.175), calls=%async_computation.2 | async-start | bytes 1572864 | tf_op jit(solution)/shard_map/all_to_all | solution.py:26
  72.7 60.2 %all-to-all-start.4 = ((bf16[32,128,512]{2,1,0:T(8,128)(2,1)}), bf16[32,128,512]{2,1,0:T(8,128)(2,1)}, u32[]{:S(2)}, u32[]{:S(2)}) async-start(bf16[32,128,512]{2,1,0:T(8,128)(2,1)} %stack.3), calls=%async_computation.4 | async-start | bytes 8388608 | tf_op jit(solution)/shard_map/all_to_all | solution.py:55
  80.2 410.8 %reduce-scatter.3.cloned.1.call-start = ((), (), s32[]{:S(2)}) async-start(), calls=%async_computation.11 | async-start | bytes 4325376 | tf_op jit(solution)/shard_map/reduce_scatter | solution.py:184
  81.8 10.7 %collective-permute-start = (bf16[384,512]{1,0:T(8,128)(2,1)}, bf16[384,512]{1,0:T(8,128)(2,1)}, u32[]{:S(2)}, u32[]{:S(2)}) collective-permute-start(bf16[384,512]{1,0:T(8,128)(2,1)} %bitcast.2), channel_id=1, source_target_pairs={{0,4},{4,8},{8,12},{12,16},{16,20},{20,24},{24,28},{28,32},{32,36}... | collective-permute-start | bytes 1179656 | tf_op jit(solution)/shard_map/ppermute | solution.py:18
  85.4 8.7 %collective-permute-start.1 = (bf16[384,512]{1,0:T(8,128)(2,1)}, bf16[384,512]{1,0:T(8,128)(2,1)S(1)}, u32[]{:S(2)}, u32[]{:S(2)}) collective-permute-start(bf16[384,512]{1,0:T(8,128)(2,1)} %bitcast.13), channel_id=1, source_target_pairs={{0,4},{4,8},{8,12},{12,16},{16,20},{20,24},{24,28},{28,32},{32,36}... | collective-permute-start | bytes 1179656 | tf_op jit(solution)/shard_map/ppermute | solution.py:18
  93.9 5.6 copy-start.14
  151.7 5.9 copy-start.12
  153.0 4.9 copy-start.10
  158.1 6.7 %copy-start.7 = (bf16[2048,4,128]{2,0,1:T(8,128)(2,1)}, bf16[2048,4,128]{2,0,1:T(8,128)(2,1)S(1)}, u32[]{:S(2)}) copy-start(bf16[2048,4,128]{2,0,1:T(8,128)(2,1)S(1)} %constant_dynamic-update-slice_fusion.5) | copy-start | bytes 6291460 | tf_op jit(solution)/shard_map/while
  179.3 4.2 copy-start.4
  183.5 4.8 copy-start.13
  188.3 5.9 copy-start.12
  189.6 4.9 copy-start.10
  194.7 6.7 %copy-start.7 = (bf16[2048,4,128]{2,0,1:T(8,128)(2,1)}, bf16[2048,4,128]{2,0,1:T(8,128)(2,1)S(1)}, u32[]{:S(2)}) copy-start(bf16[2048,4,128]{2,0,1:T(8,128)(2,1)S(1)} %constant_dynamic-update-slice_fusion.5) | copy-start | bytes 6291460 | tf_op jit(solution)/shard_map/while
  220.1 4.8 copy-start.13
  224.8 5.9 copy-start.12
  226.2 4.9 copy-start.10
  231.3 6.7 %copy-start.7 = (bf16[2048,4,128]{2,0,1:T(8,128)(2,1)}, bf16[2048,4,128]{2,0,1:T(8,128)(2,1)S(1)}, u32[]{:S(2)}) copy-start(bf16[2048,4,128]{2,0,1:T(8,128)(2,1)S(1)} %constant_dynamic-update-slice_fusion.5) | copy-start | bytes 6291460 | tf_op jit(solution)/shard_map/while
  252.5 4.2 copy-start.4
  256.6 4.8 copy-start.13
  261.4 5.9 copy-start.12
  262.7 4.9 copy-start.10
  267.9 6.7 %copy-start.7 = (bf16[2048,4,128]{2,0,1:T(8,128)(2,1)}, bf16[2048,4,128]{2,0,1:T(8,128)(2,1)S(1)}, u32[]{:S(2)}) copy-start(bf16[2048,4,128]{2,0,1:T(8,128)(2,1)S(1)} %constant_dynamic-update-slice_fusion.5) | copy-start | bytes 6291460 | tf_op jit(solution)/shard_map/while
  293.2 4.8 copy-start.13
  298.0 5.9 copy-start.12
  299.3 4.9 copy-start.10
  304.4 6.7 %copy-start.7 = (bf16[2048,4,128]{2,0,1:T(8,128)(2,1)}, bf16[2048,4,128]{2,0,1:T(8,128)(2,1)S(1)}, u32[]{:S(2)}) copy-start(bf16[2048,4,128]{2,0,1:T(8,128)(2,1)S(1)} %constant_dynamic-update-slice_fusion.5) | copy-start | bytes 6291460 | tf_op jit(solution)/shard_map/while
  329.8 4.8 copy-start.13
  334.6 5.9 copy-start.12
  335.9 4.9 copy-start.10
  341.0 6.7 %copy-start.7 = (bf16[2048,4,128]{2,0,1:T(8,128)(2,1)}, bf16[2048,4,128]{2,0,1:T(8,128)(2,1)S(1)}, u32[]{:S(2)}) copy-start(bf16[2048,4,128]{2,0,1:T(8,128)(2,1)S(1)} %constant_dynamic-update-slice_fusion.5) | copy-start | bytes 6291460 | tf_op jit(solution)/shard_map/while
  366.4 4.8 copy-start.13
  377.3 4.3 copy-start.11
  393.8 182.5 %reduce-scatter.5.cloned.1.call-start = ((), (), s32[]{:S(2)}) async-start(), calls=%async_computation.12 | async-start | bytes 4325376 | tf_op jit(solution)/shard_map/reduce_scatter | solution.py:190
  420.5 11.2 %copy-start.21 = (s32[3]{0:T(128)S(1)}, s32[3]{0:T(128)}, u32[]{:S(2)}) copy-start(s32[3]{0:T(128)} %constant.137.clone.1) | copy-start | bytes 40
  420.5 21.2 %all-to-all-start.6 = ((bf16[4,192,512]{2,1,0:T(8,128)(2,1)}), bf16[4,192,512]{2,1,0:T(8,128)(2,1)}, u32[]{:S(2)}, u32[]{:S(2)}) async-start(bf16[4,192,512]{2,1,0:T(8,128)(2,1)} %all_to_all.120), calls=%async_computation.6 | async-start | bytes 1572864 | tf_op jit(solution)/shard_map/all_to_all | solution.py:215
  427.0 19.4 %collective-permute-start.3 = (bf16[384,512]{1,0:T(8,128)(2,1)}, bf16[384,512]{1,0:T(8,128)(2,1)S(1)}, u32[]{:S(2)}, u32[]{:S(2)}) collective-permute-start(bf16[384,512]{1,0:T(8,128)(2,1)} %copy.157), channel_id=1, source_target_pairs={{4,0},{8,4},{12,8},{16,12},{20,16},{24,20},{28,24},{32,28},{36,32}... | collective-permute-start | bytes 1179656 | tf_op jit(solution)/shard_map/ppermute | solution.py:18
  430.4 19.4 %collective-permute-start.2 = (bf16[384,512]{1,0:T(8,128)(2,1)}, bf16[384,512]{1,0:T(8,128)(2,1)}, u32[]{:S(2)}, u32[]{:S(2)}) collective-permute-start(bf16[384,512]{1,0:T(8,128)(2,1)} %copy.155), channel_id=1, source_target_pairs={{4,0},{8,4},{12,8},{16,12},{20,16},{24,20},{28,24},{32,28},{36,32}... | collective-permute-start | bytes 1179656 | tf_op jit(solution)/shard_map/ppermute | solution.py:18
  441.7 137.4 %all-to-all-start.5 = ((bf16[4,192,512]{2,1,0:T(8,128)(2,1)}), bf16[4,192,512]{2,1,0:T(8,128)(2,1)}, u32[]{:S(2)}, u32[]{:S(2)}) async-start(bf16[4,192,512]{2,1,0:T(8,128)(2,1)} %all_to_all.116), calls=%async_computation.5 | async-start | bytes 1572864 | tf_op jit(solution)/shard_map/all_to_all | solution.py:214
  579.1 15.1 %all-to-all-start.7 = ((bf16[4,192,512]{2,1,0:T(8,128)(2,1)}), bf16[4,192,512]{2,1,0:T(8,128)(2,1)S(1)}, u32[]{:S(2)}, u32[]{:S(2)}) async-start(bf16[4,192,512]{2,1,0:T(8,128)(2,1)} %bitcast.176), calls=%async_computation.8 | async-start | bytes 1572864 | tf_op jit(solution)/shard_map/all_to_all | solution.py:216
  594.2 13.0 %all-to-all-start.8 = ((bf16[4,192,512]{2,1,0:T(8,128)(2,1)}), bf16[4,192,512]{2,1,0:T(8,128)(2,1)S(1)}, u32[]{:S(2)}, u32[]{:S(2)}) async-start(bf16[4,192,512]{2,1,0:T(8,128)(2,1)} %bitcast.31), calls=%async_computation.10 | async-start | bytes 1572864 | tf_op jit(solution)/shard_map/all_to_all | solution.py:217
  (50 other events, 131.4 us)
Sparse Core Ops, SparseCore 0:
  28.0 45.4 all-gather.2
  393.9 97.0 reduce-scatter.2
  495.1 81.1 reduce-scatter.4
